TPU v7x, 32 devices: a whole 2x2x4 slice. The times are simulated.
32 devices in a mesh: group: 2 (over x), dp: 16 (over z, y, core).
Axes of the slice: x: 2, y: 2, z: 4, core: 2. Of those that a mesh axis runs over, the one named last changes fastest.
Arguments:
- acts: bfloat16 [2, 8192, 4096], P(None, ('group', 'dp')), parts along dimension 1, may hold values from -16 to 16
- grads: bfloat16 [2, 8192, 4096], P(None, ('group', 'dp')), parts along dimension 1, may hold values from -16 to 16
- proj_in: bfloat16 [2, 4096, 64], replicated, may hold values from -0.09375 to 0.09375
- proj_out: bfloat16 [2, 4096, 64], replicated, may hold values from -0.09375 to 0.09375
- example_ids: int32 [32, 256], P(('group', 'dp')), parts along dimension 0, may hold values from 0 to 15, never falling along the last dimension, each value on 1 to 32 neighbouring positions
- queries: bfloat16 [2, 256, 4096], P(None, 'dp'), may hold values from -6 to 6
Outputs:
- scores: float32 [512, 256], P(('group', 'dp')), parts along dimension 0
There are 2 independent parts, one for each index of `group`. A program takes and returns all parts, laid end to end along the dimension named above; an argument that names none is the same for every part. Nothing has to cross between parts.
Inputs may be any that keep to these rules, and one draw needn't show every extreme that they name: `example_ids`: each row is non-decreasing, every number 0 to 15 appears, each example has 1 to 32 tokens, one exactly that many.
All inputs are finite; a program needn't handle non-finite values.
Results may differ from a plain program's by a relative error of at most 0.0003.
Values may be sent and summed in bfloat16 or wider, within the bound.
A program may use at most 128 MiB of HBM per device.

v0:
```python
import jax
import jax.numpy as jnp
from jax import lax
from jax.sharding import PartitionSpec as P

EX_DEV = 16


def invert_damped(factor):
    width = factor.shape[0]
    identity = jnp.eye(width, dtype=jnp.float32)
    damped = factor + 0.1 * (jnp.trace(factor) / width) * identity
    lower = jnp.linalg.cholesky(damped)
    return jax.scipy.linalg.cho_solve((lower, True), identity)


def shards(acts, grads, proj_in, proj_out, example_ids, queries):
    highest = lax.Precision.HIGHEST
    layers = acts.shape[0]
    width = proj_in.shape[2]
    total_tokens = acts.shape[1] * lax.axis_size("dp")
    onehot = (example_ids[0][None, :] == jnp.arange(EX_DEV, dtype=jnp.int32)[:, None]).astype(
        jnp.float32
    )
    act_sums = []
    grad_sums = []
    example_list = []
    for layer in range(layers):
        inner = jnp.dot(acts[layer], proj_in[layer], preferred_element_type=jnp.float32)
        outer = jnp.dot(grads[layer], proj_out[layer], preferred_element_type=jnp.float32)
        act_part = jnp.dot(inner.T, inner, precision=highest)
        grad_part = jnp.dot(outer.T, outer, precision=highest)
        act_sums.append(act_part)
        grad_sums.append(grad_part)
        weighted = onehot[:, :, None] * outer[None, :, :]
        example_list.append(jnp.einsum("etr,ti->eri", weighted, inner, precision=highest))
    act_stack = jnp.stack(act_sums)
    grad_stack = jnp.stack(grad_sums)
    act_stack, grad_stack = lax.psum((act_stack, grad_stack), "dp")
    inv_act = jax.vmap(invert_damped)(act_stack / total_tokens)
    inv_grad = jax.vmap(invert_damped)(grad_stack / total_tokens)
    example_grad = jnp.stack(example_list)
    factor_scale = 1.0 / jnp.sqrt(jnp.float32(layers * width * width))
    left = jnp.einsum("lij,lejk->leik", inv_grad, example_grad, precision=highest)
    whitened = jnp.einsum("leik,lkm->leim", left, inv_act, precision=highest)
    flat_examples = whitened.reshape(layers, EX_DEV, width * width)
    return (
        jnp.einsum(
            "lnk,lek->en",
            lax.all_gather(queries, "dp", axis=1, tiled=True).astype(jnp.float32),
            flat_examples,
            precision=highest,
        )
        * factor_scale
    )


def solution(mesh):
    return jax.shard_map(
        shards,
        mesh=mesh,
        in_specs=(
            P(None, ("group", "dp"), None),
            P(None, ("group", "dp"), None),
            P(),
            P(),
            P(("group", "dp"), None),
            P(None, "dp", None),
        ),
        out_specs=P(("group", "dp"), None),
        check_vma=False,
    )
```

profile of v0, /device:TPU:1, one launch (start us, length us, event | category | flops | bytes accessed | tf_op | source)
XLA Modules:
  0.0 172.5 jit_solution(9589441344956510345)
XLA Ops:
  6.5 2.6 %fusion = f32[256,64]{0,1:T(8,128)S(1)} fusion(bf16[2,256,4096]{2,1,0:T(8,128)(2,1)} %param.9, bf16[2,4096,64]{1,2,0:T(8,128)(2,1)} %param.11), kind=kOutput, calls=%fused_computation | convolution fusion | flops 134217728 | bytes 2686976 | tf_op jit(solution)/shard_map/dot_general | solution.py:29
  9.1 2.4 %fusion.4 = f32[256,64]{0,1:T(8,128)S(1)} fusion(bf16[2,256,4096]{2,1,0:T(8,128)(2,1)} %param.9, bf16[2,4096,64]{1,2,0:T(8,128)(2,1)} %param.11), kind=kOutput, calls=%fused_computation.4 | convolution fusion | flops 134217728 | bytes 2686976 | tf_op jit(solution)/shard_map/dot_general | solution.py:29
  11.6 0.8 fusion.2
  12.4 0.8 fusion.6
  13.1 0.2 convolution_bitcast_fusion.5
  14.0 0.6 pad_maximum_fusion
  14.6 0.2 all-gather.2.cloned.1.call-start
  14.9 0.5 all-gather.2.cloned.1.call-update
  15.6 1.0 convolution_bitcast_fusion.1
  16.5 1.0 convolution_bitcast_fusion.2
  17.5 87.0 %all-reduce.3.cloned.1.call-done = (f32[2,64,64]{1,2,0:T(8,128)}, f32[2,64,64]{1,2,0:T(8,128)}) async-done(((f32[2,64,64]{1,2,0:T(8,128)}, f32[2,64,64]{1,2,0:T(8,128)}), (f32[2,64,64]{1,2,0:T(8,128)}, f32[2,64,64]{1,2,0:T(8,128)})) %all-reduce.3.cloned.1.call-update) | async-done | bytes 65552 | tf_op jit(solution)/shard_map/psum | solution.py:39
  104.5 1.0 select_reduce_fusion.2
  105.5 1.0 multiply_add_fusion
  106.6 11.7 %custom-call.10 = f32[2,64,64]{2,1,0:T(8,128)S(1)} custom-call(f32[2,64,64]{2,1,0:T(8,128)S(1)} %fusion.37), custom_call_target="Cholesky" | custom-call | tf_op jit(solution)/shard_map/vmap(jit(cholesky))/cholesky | solution.py:13
  118.4 11.7 %custom-call.12 = f32[2,64,64]{2,1,0:T(8,128)S(1)} custom-call(f32[2,64,64]{2,1,0:T(8,128)S(1)} %fusion.33), custom_call_target="Cholesky" | custom-call | tf_op jit(solution)/shard_map/vmap(jit(cholesky))/cholesky | solution.py:13
  130.6 9.8 %custom-call.11 = f32[2,1,64,64]{2,3,1,0:T(8,128)S(1)} custom-call(f32[2,1,64,64]{3,2,1,0:T(8,128)S(1)} %get-tuple-element.16), custom_call_target="InvertDiagBlocksLowerTriangular" | custom-call | tf_op jit(solution)/shard_map/vmap(jit(_cho_solve))/triangular_solve | solution.py:14
  140.4 9.8 %custom-call.13 = f32[2,1,64,64]{2,3,1,0:T(8,128)S(1)} custom-call(f32[2,1,64,64]{3,2,1,0:T(8,128)S(1)} %get-tuple-element.15), custom_call_target="InvertDiagBlocksLowerTriangular" | custom-call | tf_op jit(solution)/shard_map/vmap(jit(_cho_solve))/triangular_solve | solution.py:14
  150.2 0.3 fusion.35
  150.7 0.3 fusion.31
  151.2 1.1 convolution_bitcast_fusion
  152.4 1.0 fusion.45
  153.4 0.4 reshape.51
  153.7 5.7 %all-gather.2.cloned.1.call-done = bf16[2,256,4096]{2,1,0:T(8,128)(2,1)} async-done(((bf16[2,16,4096]{2,1,0:T(8,128)(2,1)}), bf16[2,256,4096]{2,1,0:T(8,128)(2,1)}) %all-gather.2.cloned.1.call-update) | async-done | bytes 4194320 | tf_op jit(solution)/shard_map/all_gather | solution.py:50
  159.5 6.1 %fusion.12 = f32[16,256]{1,0:T(8,128)} fusion(f32[2,16,4096]{2,1,0:T(8,128)S(1)} %reshape.51, bf16[2,256,4096]{2,1,0:T(8,128)(2,1)} %all-gather.2.cloned.1.call-done), kind=kOutput, calls=%fused_computation.22 | convolution fusion | flops 402657280 | bytes 4734976 | tf_op jit(solution)/shard_map/lnk,lek->en/dot_general | solution.py:48
  (29 shorter events, 1.7 us)
Async XLA Ops:
  6.5 5.0 %copy-start.2 = (bf16[2,4096,64]{1,2,0:T(8,128)(2,1)S(1)}, bf16[2,4096,64]{1,2,0:T(8,128)(2,1)}, u32[]{:S(2)}) copy-start(bf16[2,4096,64]{1,2,0:T(8,128)(2,1)} %param.12) | copy-start | bytes 3145732
  6.5 98.0 %all-reduce.3.cloned.1.call-start = ((), (), s32[]{:S(2)}) async-start(), calls=%async_computation.1 | async-start | bytes 262144 | tf_op jit(solution)/shard_map/psum | solution.py:39
  6.5 5.0 %copy-start.1 = (bf16[2,256,4096]{2,1,0:T(8,128)(2,1)S(1)}, bf16[2,256,4096]{2,1,0:T(8,128)(2,1)}, u32[]{:S(2)}) copy-start(bf16[2,256,4096]{2,1,0:T(8,128)(2,1)} %param.10) | copy-start | bytes 12582916
  11.6 4.0 %copy-start = (s32[1,256]{1,0:T(1,128)S(1)}, s32[1,256]{1,0:T(1,128)}, u32[]{:S(2)}) copy-start(s32[1,256]{1,0:T(1,128)} %param.13) | copy-start | bytes 3076
  14.6 144.8 %all-gather.2.cloned.1.call-start = ((), (), s32[]{:S(2)}) async-start(), calls=%async_computation | async-start | bytes 4456448 | tf_op jit(solution)/shard_map/all_gather | solution.py:50
Sparse Core Ops, SparseCore 0:
  14.8 89.7 all-reduce.2
  106.7 52.6 all-gather.1
where the time goes:
time: 173 us; the launch traced here: 172 us
  waiting for transfers between devices  93.3 us (54%)
  other arithmetic  46.2 us (27%)
  matrix products  18.6 us (11%)
  between operations  13.6 us (8%)
    psum x1, waiting for transfers between devices, shards(): act_stack, grad_stack = lax.psum((act_stack, grad_stack), 'dp')  87 us
    another operation x6, other arithmetic, invert_damped(): lower = jnp.linalg.cholesky(damped)  23.7 us
    another operation x4, other arithmetic, invert_damped(): return jax.scipy.linalg.cho_solve((lower, True), identity)  19.8 us
    dot_general x1, matrix products, shards(): jnp.einsum('lnk,lek->en', lax.all_gather(queries, 'dp', axis=1, tiled=Tru...  6.15 us
    all_gather x1, waiting for transfers between devices, shards(): lax.all_gather(queries, 'dp', axis=1, tiled=True).astype(jnp.float32)  5.72 us
    dot_general x2, matrix products, shards(): jnp.dot(acts[layer], proj_in[layer], preferred_element_type=jnp.float32)  5.01 us
  transfers between devices with their start and end apart: 2, of which 2 were waited for; matrix products, arithmetic and copies ran while one was open for 30% of the time, Pallas kernels for 0%

commit v1 on v0

v1 whole, which is shorter than its diff:
```python
import functools

import jax
import jax.numpy as jnp
from jax import lax
from jax.experimental import pallas as pl
from jax.experimental.pallas import tpu as pltpu
from jax.sharding import PartitionSpec as P

EX_DEV = 16
SLICES = 16
DAMP = 0.1
MESH = pl.DeviceIdType.MESH
HIGHEST = lax.Precision.HIGHEST
NT = (((1,), (1,)), ((), ()))
TN = (((0,), (0,)), ((), ()))


def split(x):
    hi = x.astype(jnp.bfloat16)
    return hi, (x - hi.astype(jnp.float32)).astype(jnp.bfloat16)


def dot(a, b):
    return jnp.dot(a, b, precision=HIGHEST, preferred_element_type=jnp.float32)


def bdot(a, b):
    return jnp.dot(a, b, preferred_element_type=jnp.float32)


def kernel(
    n, folded, acts, grads, pin, pout, ids, queries, out,
    abuf, pbuf, qbuf, gram, rsbuf, xbuf, full,
    load_sem, own_sem, rs_send, rs_recv, x_send, x_recv, ag_send, ag_recv,
    ring_send, ring_recv, chip_send, chip_recv,
):
    layers, tokens, _ = acts.shape
    width = pin.shape[1]
    me = lax.axis_index("dp")
    chips = n // 2
    half = chips // 2
    chip, core = me // 2, me % 2

    def pos_to_dev(p):
        p = (p + chips) % chips
        if folded:
            y = p // half
            z = p * (1 - y) + (chips - 1 - p) * y
            p = 2 * z + y
        return 2 * p + core

    if folded:
        z, y = chip // 2, chip % 2
        pos = z + y * (chips - 1 - 2 * z)
    else:
        pos = chip
    right, left = pos_to_dev(pos + 1), pos_to_dev(pos - 1)
    partner = 2 * chip + (1 - core)

    barrier = pltpu.get_barrier_semaphore()
    for k in range(1, n):
        pl.semaphore_signal(barrier, inc=1, device_id={"dp": (me + k) % n}, device_id_type=MESH)

    loads = []
    for layer in range(layers):
        for side, (data, proj) in enumerate(((acts, pin), (grads, pout))):
            i = 2 * layer + side
            loads.append((
                pltpu.make_async_copy(proj.at[layer], pbuf.at[i], load_sem.at[2 * i]),
                pltpu.make_async_copy(data.at[layer], abuf.at[i], load_sem.at[2 * i + 1]),
            ))
            for copy in loads[-1]:
                copy.start()

    def rows(dev):
        return pl.ds(pl.multiple_of(dev * EX_DEV, EX_DEV), EX_DEV)

    def remote(src, dst, send, recv, dev):
        return pltpu.make_async_remote_copy(
            src_ref=src, dst_ref=dst, send_sem=send, recv_sem=recv,
            device_id={"dp": dev}, device_id_type=MESH,
        )

    def ring(step, way, arriving):
        sign = 1 - 2 * way
        origin = pos_to_dev(pos - sign * (step + (1 if arriving else 0)))
        lay = slice(None) if step < half - 1 else pl.ds(way, 1)
        dst = qbuf.at[lay, rows(origin), :]
        src = queries.at[lay] if step == 0 and not arriving else dst
        return remote(src, dst, ring_send.at[way, step], ring_recv.at[way, step], right if way == 0 else left)

    def on_chip(index, step, way, arriving):
        if index == 0:
            lay, origin = slice(None), me
        else:
            lay = slice(None) if step < half - 1 else pl.ds(way, 1)
            sign = 1 - 2 * way
            origin = pos_to_dev(pos - sign * (step + 1))
        if arriving:
            origin = origin + (1 - 2 * core)
        dst = qbuf.at[lay, rows(origin), :]
        src = queries if index == 0 and not arriving else dst
        return remote(src, dst, chip_send.at[index], chip_recv.at[index], partner)

    def advance(step):
        for way in range(2):
            ring(step, way, True).wait_recv()
            if step + 1 < half:
                ring(step + 1, way, False).start()
            on_chip(1 + 2 * step + way, step, way, False).start()

    pl.semaphore_wait(barrier, n - 1)
    for way in range(2):
        ring(0, way, False).start()
    on_chip(0, 0, 0, False).start()
    own = pltpu.make_async_copy(queries, qbuf.at[:, rows(me), :], own_sem)
    own.start()

    lane = lax.broadcasted_iota(jnp.int32, (1, 2 * width), 1)
    low = lane < width
    tokens_out = []
    for layer in range(layers):
        sides = []
        for side in range(2):
            i = 2 * layer + side
            for copy in loads[i]:
                copy.wait()
            sides.append(lax.dot_general(abuf[i], pbuf[i], NT, preferred_element_type=jnp.float32))
        both = jnp.concatenate(sides, axis=1)
        tokens_out.append(both)
        g = lax.dot_general(both, both, TN, precision=HIGHEST, preferred_element_type=jnp.float32)
        gram[pl.ds(layer * width, width), :] = jnp.where(low, g[:width], g[width:])

    slot = me % SLICES
    block = me - slot

    def slice_of(ref, s):
        return ref.at[pl.ds(pl.multiple_of(8 * s, 8), 8), :]

    peers = [(slot + k) % SLICES for k in range(SLICES)]
    sources = [(slot + SLICES - k) % SLICES for k in range(SLICES)]
    scatter = [
        remote(slice_of(gram, peers[k]), rsbuf.at[k], rs_send.at[k], rs_recv.at[k], block + peers[k])
        for k in range(1, SLICES)
    ]
    for copy in scatter:
        copy.start()
    mine = gram[pl.ds(pl.multiple_of(8 * slot, 8), 8), :]
    advance(0)
    for copy in scatter:
        copy.wait_recv()
    for k in range(1, SLICES):
        mine = mine + rsbuf[k]
    blocks = n // SLICES
    crossing = []
    if blocks > 1:
        xbuf[0] = mine
        for k in range(1, blocks):
            copy = remote(xbuf.at[0], xbuf.at[k], x_send.at[k], x_recv.at[k], (me + k * SLICES) % n)
            copy.start()
            crossing.append(copy)
        for copy in crossing:
            copy.wait_recv()
        home = me // SLICES
        mine = jnp.zeros_like(mine)
        for b in range(blocks):
            mine = mine + xbuf[(home - b + blocks) % blocks]
    full[pl.ds(pl.multiple_of(8 * slot, 8), 8), :] = mine
    gather = [
        remote(slice_of(full, slot), slice_of(full, slot), ag_send.at[k], ag_recv.at[k], block + peers[k])
        for k in range(1, SLICES)
    ]
    for copy in gather:
        copy.start()
    for k in range(1, SLICES):
        there = slice_of(full, sources[k])
        remote(there, there, ag_send.at[k], ag_recv.at[k], block + sources[k]).wait_recv()

    wide = 2 * width
    row = lax.broadcasted_iota(jnp.int32, (wide, wide), 0)
    col = lax.broadcasted_iota(jnp.int32, (wide, wide), 1)
    eye = (row == col).astype(jnp.float32)
    same = (row < width) == (col < width)
    total_tokens = tokens * n
    top, bottom = width + DAMP, DAMP
    mats, scales = [], []
    for layer in range(layers):
        f = full[pl.ds(layer * width, width), :]
        f = jnp.where(same, jnp.concatenate([f, f], axis=0), 0.0) / total_tokens
        diag = jnp.sum(f * eye, axis=0, keepdims=True)
        first = jnp.sum(jnp.where(low, diag, 0.0), axis=1, keepdims=True)
        second = jnp.sum(jnp.where(low, 0.0, diag), axis=1, keepdims=True)
        inv = width / jnp.where(low, first, second)
        scales.append(inv)
        mats.append(f * inv + DAMP * eye)
    t = (top + bottom) / (top - bottom)
    rs = [eye - m * (2.0 / (top + bottom)) for m in mats]
    xs = None
    for doubling in range(7):
        t2 = 2.0 * t * t - 1.0
        up = 2.0 * t * t / t2
        if doubling == 0:
            xs = [(eye + r) * (up * 2.0 / (top + bottom)) for r in rs]
        else:
            xs = [(x + dot(x, r)) * up for x, r in zip(xs, rs)]
        if doubling < 6:
            rs = [dot(r, r) * up - eye * (1.0 / t2) for r in rs]
        t = t2
    advance(1)
    xs = [x + dot(x, eye - dot(m, x)) for m, x in zip(mats, xs)]
    xs = [x * inv for x, inv in zip(xs, scales)]

    onehot = (ids[...] == lax.broadcasted_iota(jnp.int32, (EX_DEV, tokens), 0)).astype(jnp.float32)
    flat = []
    for layer in range(layers):
        w = dot(tokens_out[layer], xs[layer])
        twice = jnp.where(low, w, pltpu.roll(w, width, 1))
        o = w.T[width:]
        rhi, rlo = split(twice)
        lhs = (o[:, None, :] * onehot[None, :, :]).reshape(width * EX_DEV, tokens)
        lhi, llo = split(lhs)
        p = bdot(lhi, rhi) + bdot(lhi, rlo) + bdot(llo, rhi)
        p = p.reshape(width // 2, 2, EX_DEV, wide)
        p = jnp.where(low[None], p[:, 0], p[:, 1])
        p = jnp.concatenate([p[m] for m in range(width // 2)], axis=1)
        hi, lo = split(p)
        flat.append(jnp.concatenate([hi, lo], axis=0))

    for step in range(2, half):
        advance(step)
    own.wait()
    for index in range(2 * half + 1):
        step, way = max(index - 1, 0) // 2, max(index - 1, 0) % 2
        on_chip(index, step, way, True).wait_recv()
    acc = jnp.zeros((2 * EX_DEV, EX_DEV * n), jnp.float32)
    for layer in range(layers):
        acc = acc + lax.dot_general(flat[layer], qbuf[layer], NT, preferred_element_type=jnp.float32)
    out[...] = acc[:EX_DEV] + acc[EX_DEV:]

    for copy in scatter + crossing + gather:
        copy.wait_send()
    for step in range(half):
        for way in range(2):
            ring(step, way, False).wait_send()
    for index in range(2 * half + 1):
        step, way = max(index - 1, 0) // 2, max(index - 1, 0) % 2
        on_chip(index, step, way, False).wait_send()


def shards(n, acts, grads, proj_in, proj_out, example_ids, queries):
    layers, tokens, depth = acts.shape
    width = proj_in.shape[2]
    half = n // 4
    any_spec = pl.BlockSpec(memory_space=pl.ANY)
    vmem = pl.BlockSpec(memory_space=pltpu.VMEM)
    dma = pltpu.SemaphoreType.DMA
    sums = pl.pallas_call(
        functools.partial(kernel, n, n == 16),
        out_shape=jax.ShapeDtypeStruct((EX_DEV, EX_DEV * n), jnp.float32),
        in_specs=[any_spec] * 4 + [vmem, any_spec],
        out_specs=vmem,
        scratch_shapes=[
            pltpu.VMEM((2 * layers, tokens, depth), jnp.bfloat16),
            pltpu.VMEM((2 * layers, width, depth), jnp.bfloat16),
            pltpu.VMEM((layers, EX_DEV * n, width * width), jnp.bfloat16),
            pltpu.VMEM((layers * width, 2 * width), jnp.float32),
            pltpu.VMEM((SLICES, 8, 2 * width), jnp.float32),
            pltpu.VMEM((max(n // SLICES, 1), 8, 2 * width), jnp.float32),
            pltpu.VMEM((layers * width, 2 * width), jnp.float32),
            dma((4 * layers,)),
            dma,
            dma((SLICES,)), dma((SLICES,)),
            dma((n // SLICES,)), dma((n // SLICES,)),
            dma((SLICES,)), dma((SLICES,)),
            dma((2, half)), dma((2, half)),
            dma((2 * half + 1,)), dma((2 * half + 1,)),
        ],
        compiler_params=pltpu.CompilerParams(
            collective_id=0, has_side_effects=True, vmem_limit_bytes=60 * 1024 * 1024
        ),
        name="influence",
    )(
        acts, grads, proj_in.transpose(0, 2, 1), proj_out.transpose(0, 2, 1), example_ids, queries,
    )
    return sums * (1.0 / jnp.sqrt(jnp.float32(layers * width * width)))


def solution(mesh):
    return jax.shard_map(
        functools.partial(shards, mesh.shape["dp"]),
        mesh=mesh,
        in_specs=(
            P(None, ("group", "dp"), None),
            P(None, ("group", "dp"), None),
            P(),
            P(),
            P(("group", "dp"), None),
            P(None, "dp", None),
        ),
        out_specs=P(("group", "dp"), None),
        check_vma=False,
    )
```

time: 173 us -> 44.6 us (0.26)
  waiting for transfers between devices: 93.3 us -> 0 us
  other arithmetic: 46.2 us -> 1.33 us
  Pallas kernels: 0 us -> 43 us
  matrix products: 18.6 us -> 0 us
  between operations: 13.6 us -> 0.01 us
    psum x1 -> x0, waiting for transfers between devices: 87 us -> none  [shards(): act_stack, grad_stack = lax.psum((act_stack, grad_stack), 'dp')]
    another operation x11 -> x0, other arithmetic: 44.2 us -> none  [the longest x6 23.7 us: invert_damped(): lower = jnp.linalg.cholesky(damped)]
    pallas_call x0 -> x1, Pallas kernels: none -> 43 us  [shards(): pl.pallas_call(functools.partial(kernel, n, n == 16), out_shape=jax.Shape...]
    dot_general x13 -> x0, matrix products: 17.6 us -> none  [the longest x1 6.15 us: shards(): jnp.einsum('lnk,lek->en', lax.all_gather(queries, 'dp', axis=1, tiled=Tru...]
    all_gather x1 -> x0, waiting for transfers between devices: 5.72 us -> none  [shards(): lax.all_gather(queries, 'dp', axis=1, tiled=True).astype(jnp.float32)]
  transfers between devices with their start and end apart: 2 -> 0, of which waited for: 2 -> 0; matrix products, arithmetic and copies ran while one was open for 30% -> 0% of each run, Pallas kernels for 0% -> 0%
where the time goes in v1:
time: 44.6 us; the launch traced here: 44.3 us
  Pallas kernels  43 us (96%)
  other arithmetic  1.33 us (3%)
    pallas_call x1, Pallas kernels, shards(): pl.pallas_call(functools.partial(kernel, n, n == 16), out_shape=jax.Shape...  43 us
    mul x1, other arithmetic, shards(): return sums * (1.0 / jnp.sqrt(jnp.float32(layers * width * width)))  1.33 us

profile of v1, /device:TPU:1, one launch (start us, length us, event | category | flops | bytes accessed | tf_op | source)
XLA Modules:
  0.0 44.3 jit_solution(2921515032981356251)
XLA Ops:
  0.0 43.0 %influence.1 = f32[16,256]{1,0:T(8,128)} custom-call(bf16[2,256,4096]{2,1,0:T(8,128)(2,1)} %acts.1, bf16[2,256,4096]{2,1,0:T(8,128)(2,1)} %grads.1, bf16[2,64,4096]{2,1,0:T(8,128)(2,1)} %bitcast.2, bf16[2,64,4096]{2,1,0:T(8,128)(2,1)} %bitcast.3, s32[1,256]{1,0:T(1,128)} %ids.1, bf16[2,16,4096]{2,1,0:T(8,128)(2,1)} %queries.1), custom_call_target="tpu_custom_call" | custom-call | tf_op jit(solution)/shard_map/influence/pallas_call | solution.py:258
  43.0 1.3 %broadcast_multiply_fusion = f32[16,256]{1,0:T(8,128)} fusion(f32[16,256]{1,0:T(8,128)} %influence.1), kind=kLoop, calls=%fused_computation | loop fusion | flops 4096 | bytes 32768 | tf_op jit(solution)/shard_map/mul | solution.py:286

commit v2 on v1

--- a/solution.py
+++ b/solution.py
@@ -31,11 +31,12 @@
 
 def kernel(
     n, folded, acts, grads, pin, pout, ids, queries, out,
-    abuf, pbuf, qbuf, gram, rsbuf, xbuf, full,
+    abuf, pbuf, qbuf, gram, rsbuf, xbuf, full, xs, rs, outer_t, inner_2, flat,
     load_sem, own_sem, rs_send, rs_recv, x_send, x_recv, ag_send, ag_recv,
     ring_send, ring_recv, chip_send, chip_recv,
 ):
-    layers, tokens, _ = acts.shape
+    layers, tokens, depth = acts.shape
+    step_k = 1024
     width = pin.shape[1]
     me = lax.axis_index("dp")
     chips = n // 2
@@ -82,55 +83,70 @@
             device_id={"dp": dev}, device_id_type=MESH,
         )
 
-    def ring(step, way, arriving):
+    def ring(step, way, layer, arriving):
         sign = 1 - 2 * way
         origin = pos_to_dev(pos - sign * (step + (1 if arriving else 0)))
-        lay = slice(None) if step < half - 1 else pl.ds(way, 1)
-        dst = qbuf.at[lay, rows(origin), :]
-        src = queries.at[lay] if step == 0 and not arriving else dst
-        return remote(src, dst, ring_send.at[way, step], ring_recv.at[way, step], right if way == 0 else left)
-
-    def on_chip(index, step, way, arriving):
-        if index == 0:
-            lay, origin = slice(None), me
-        else:
-            lay = slice(None) if step < half - 1 else pl.ds(way, 1)
-            sign = 1 - 2 * way
-            origin = pos_to_dev(pos - sign * (step + 1))
+        dst = qbuf.at[layer, rows(origin), :]
+        src = queries.at[layer] if step == 0 and not arriving else dst
+        sems = ring_send.at[way, step, layer], ring_recv.at[way, step, layer]
+        return remote(src, dst, *sems, right if way == 0 else left)
+
+    def carried(step, way):
+        if step < half - 1:
+            return list(range(layers))
+        return list(range(way, layers, 2))
+
+    def on_chip(step, way, layer, arriving):
+        sign = 1 - 2 * way
+        origin = me if step < 0 else pos_to_dev(pos - sign * (step + 1))
         if arriving:
             origin = origin + (1 - 2 * core)
-        dst = qbuf.at[lay, rows(origin), :]
-        src = queries if index == 0 and not arriving else dst
-        return remote(src, dst, chip_send.at[index], chip_recv.at[index], partner)
-
-    def advance(step):
+        dst = qbuf.at[layer, rows(origin), :]
+        src = queries.at[layer] if step < 0 and not arriving else dst
+        sems = chip_send.at[way, step + 1, layer], chip_recv.at[way, step + 1, layer]
+        return remote(src, dst, *sems, partner)
+
+    def advance(step, layer):
         for way in range(2):
-            ring(step, way, True).wait_recv()
-            if step + 1 < half:
-                ring(step + 1, way, False).start()
-            on_chip(1 + 2 * step + way, step, way, False).start()
-
-    pl.semaphore_wait(barrier, n - 1)
-    for way in range(2):
-        ring(0, way, False).start()
-    on_chip(0, 0, 0, False).start()
-    own = pltpu.make_async_copy(queries, qbuf.at[:, rows(me), :], own_sem)
-    own.start()
+            if layer in carried(step, way):
+                ring(step, way, layer, True).wait_recv()
+                if step + 1 < half and layer in carried(step + 1, way):
+                    ring(step + 1, way, layer, False).start()
+                on_chip(step, way, layer, False).start()
 
     lane = lax.broadcasted_iota(jnp.int32, (1, 2 * width), 1)
     low = lane < width
     tokens_out = []
+
+    def project(i):
+        def part(c, total):
+            at = pl.ds(pl.multiple_of(c * step_k, step_k), step_k)
+            return total + lax.dot_general(
+                abuf[i, :, at], pbuf[i, :, at], NT, preferred_element_type=jnp.float32
+            )
+
+        return lax.fori_loop(0, depth // step_k, part, jnp.zeros((tokens, width), jnp.float32))
+
     for layer in range(layers):
         sides = []
         for side in range(2):
             i = 2 * layer + side
             for copy in loads[i]:
                 copy.wait()
-            sides.append(lax.dot_general(abuf[i], pbuf[i], NT, preferred_element_type=jnp.float32))
+            sides.append(project(i))
         both = jnp.concatenate(sides, axis=1)
         tokens_out.append(both)
         g = lax.dot_general(both, both, TN, precision=HIGHEST, preferred_element_type=jnp.float32)
         gram[pl.ds(layer * width, width), :] = jnp.where(low, g[:width], g[width:])
+
+    pl.semaphore_wait(barrier, n - 1)
+    for layer in range(layers):
+        for way in range(2):
+            ring(0, way, layer, False).start()
+    for layer in range(layers):
+        on_chip(-1, 0, layer, False).start()
+    own = pltpu.make_async_copy(queries, qbuf.at[:, rows(me), :], own_sem)
+    own.start()
 
     slot = me % SLICES
     block = me - slot
@@ -147,7 +163,8 @@
     for copy in scatter:
         copy.start()
     mine = gram[pl.ds(pl.multiple_of(8 * slot, 8), 8), :]
-    advance(0)
+    advance(0, 0)
+    advance(0, 1)
     for copy in scatter:
         copy.wait_recv()
     for k in range(1, SLICES):
@@ -173,10 +190,12 @@
     ]
     for copy in gather:
         copy.start()
+    advance(1, 0)
     for k in range(1, SLICES):
         there = slice_of(full, sources[k])
         remote(there, there, ag_send.at[k], ag_recv.at[k], block + sources[k]).wait_recv()
 
+    advance(1, 1)
     wide = 2 * width
     row = lax.broadcasted_iota(jnp.int32, (wide, wide), 0)
     col = lax.broadcasted_iota(jnp.int32, (wide, wide), 1)
@@ -195,57 +214,81 @@
         scales.append(inv)
         mats.append(f * inv + DAMP * eye)
     t = (top + bottom) / (top - bottom)
-    rs = [eye - m * (2.0 / (top + bottom)) for m in mats]
-    xs = None
-    for doubling in range(7):
+    up = 2.0 * t * t / (2.0 * t * t - 1.0)
+    for layer in range(layers):
+        r = eye - mats[layer] * (2.0 / (top + bottom))
+        xs[layer] = (eye + r) * (up * 2.0 / (top + bottom))
+        rs[layer] = dot(r, r) * up - eye * (up - 1.0)
+
+    def doubling(_, t):
         t2 = 2.0 * t * t - 1.0
         up = 2.0 * t * t / t2
-        if doubling == 0:
-            xs = [(eye + r) * (up * 2.0 / (top + bottom)) for r in rs]
-        else:
-            xs = [(x + dot(x, r)) * up for x, r in zip(xs, rs)]
-        if doubling < 6:
-            rs = [dot(r, r) * up - eye * (1.0 / t2) for r in rs]
-        t = t2
-    advance(1)
-    xs = [x + dot(x, eye - dot(m, x)) for m, x in zip(mats, xs)]
-    xs = [x * inv for x, inv in zip(xs, scales)]
+        for layer in range(layers):
+            x, r = xs[layer], rs[layer]
+            xs[layer] = (x + dot(x, r)) * up
+            rs[layer] = dot(r, r) * up - eye * (up - 1.0)
+        return t2
+
+    lax.fori_loop(0, 6, doubling, jnp.float32(2.0 * t * t - 1.0))
+    advance(2, 0)
 
     onehot = (ids[...] == lax.broadcasted_iota(jnp.int32, (EX_DEV, tokens), 0)).astype(jnp.float32)
-    flat = []
-    for layer in range(layers):
-        w = dot(tokens_out[layer], xs[layer])
+    for layer in range(layers):
+        x, m = xs[layer], mats[layer]
+        x = (x + dot(x, eye - dot(m, x))) * scales[layer]
+        w = dot(tokens_out[layer], x)
         twice = jnp.where(low, w, pltpu.roll(w, width, 1))
-        o = w.T[width:]
-        rhi, rlo = split(twice)
-        lhs = (o[:, None, :] * onehot[None, :, :]).reshape(width * EX_DEV, tokens)
-        lhi, llo = split(lhs)
-        p = bdot(lhi, rhi) + bdot(lhi, rlo) + bdot(llo, rhi)
-        p = p.reshape(width // 2, 2, EX_DEV, wide)
-        p = jnp.where(low[None], p[:, 0], p[:, 1])
-        p = jnp.concatenate([p[m] for m in range(width // 2)], axis=1)
-        hi, lo = split(p)
-        flat.append(jnp.concatenate([hi, lo], axis=0))
-
-    for step in range(2, half):
-        advance(step)
+        inner_2[layer, 0], inner_2[layer, 1] = split(twice)
+        outer_t[layer] = w.T[width:]
+    advance(2, 1)
+
+    per = 16
+
+    def example_part(c, _):
+        for layer in range(layers):
+            o = outer_t[layer, pl.ds(pl.multiple_of(c * per, per), per), :]
+            lhs = (o[:, None, :] * onehot[None, :, :]).reshape(per * EX_DEV, tokens)
+            lhi, llo = split(lhs)
+            rhi, rlo = inner_2[layer, 0], inner_2[layer, 1]
+            p = bdot(lhi, rhi) + bdot(lhi, rlo) + bdot(llo, rhi)
+            p = p.reshape(per // 2, 2, EX_DEV, wide)
+            p = jnp.where(low[None], p[:, 0], p[:, 1])
+            p = jnp.concatenate([p[m] for m in range(per // 2)], axis=1)
+            hi, lo = split(p)
+            at = pl.ds(pl.multiple_of(c * per * width, per * width), per * width)
+            flat[layer, :, at] = jnp.concatenate([hi, lo], axis=0)
+        return 0
+
+    lax.fori_loop(0, width // per, example_part, 0)
+
+    for step in range(3, half):
+        for layer in range(layers):
+            advance(step, layer)
     own.wait()
-    for index in range(2 * half + 1):
-        step, way = max(index - 1, 0) // 2, max(index - 1, 0) % 2
-        on_chip(index, step, way, True).wait_recv()
-    acc = jnp.zeros((2 * EX_DEV, EX_DEV * n), jnp.float32)
-    for layer in range(layers):
-        acc = acc + lax.dot_general(flat[layer], qbuf[layer], NT, preferred_element_type=jnp.float32)
-    out[...] = acc[:EX_DEV] + acc[EX_DEV:]
+    everything = [(-1, 0, layer) for layer in range(layers)]
+    everything += [(step, way, layer) for step in range(half) for way in range(2) for layer in carried(step, way)]
+    for item in everything:
+        on_chip(*item, True).wait_recv()
+
+    def score_part(c, total):
+        at = pl.ds(pl.multiple_of(c * step_k, step_k), step_k)
+        for layer in range(layers):
+            total = total + lax.dot_general(
+                flat[layer, :, at], qbuf[layer, :, at], NT, preferred_element_type=jnp.float32
+            )
+        return total
+
+    total = lax.fori_loop(
+        0, width * width // step_k, score_part, jnp.zeros((2 * EX_DEV, EX_DEV * n), jnp.float32)
+    )
+    out[...] = total[:EX_DEV] + total[EX_DEV:]
 
     for copy in scatter + crossing + gather:
         copy.wait_send()
-    for step in range(half):
-        for way in range(2):
-            ring(step, way, False).wait_send()
-    for index in range(2 * half + 1):
-        step, way = max(index - 1, 0) // 2, max(index - 1, 0) % 2
-        on_chip(index, step, way, False).wait_send()
+    for item in everything:
+        if item[0] >= 0:
+            ring(*item, False).wait_send()
+        on_chip(*item, False).wait_send()
 
 
 def shards(n, acts, grads, proj_in, proj_out, example_ids, queries):
@@ -268,13 +311,18 @@
             pltpu.VMEM((SLICES, 8, 2 * width), jnp.float32),
             pltpu.VMEM((max(n // SLICES, 1), 8, 2 * width), jnp.float32),
             pltpu.VMEM((layers * width, 2 * width), jnp.float32),
+            pltpu.VMEM((layers, 2 * width, 2 * width), jnp.float32),
+            pltpu.VMEM((layers, 2 * width, 2 * width), jnp.float32),
+            pltpu.VMEM((layers, width, tokens), jnp.float32),
+            pltpu.VMEM((layers, 2, tokens, 2 * width), jnp.bfloat16),
+            pltpu.VMEM((layers, 2 * EX_DEV, width * width), jnp.bfloat16),
             dma((4 * layers,)),
             dma,
             dma((SLICES,)), dma((SLICES,)),
             dma((n // SLICES,)), dma((n // SLICES,)),
             dma((SLICES,)), dma((SLICES,)),
-            dma((2, half)), dma((2, half)),
-            dma((2 * half + 1,)), dma((2 * half + 1,)),
+            dma((2, half, layers)), dma((2, half, layers)),
+            dma((2, half + 1, layers)), dma((2, half + 1, layers)),
         ],
         compiler_params=pltpu.CompilerParams(
             collective_id=0, has_side_effects=True, vmem_limit_bytes=60 * 1024 * 1024

time: 44.6 us -> 43 us (0.964)
  Pallas kernels: 43 us -> 41.5 us
    pallas_call x1, Pallas kernels: 43 us -> 41.5 us  [shards(): pl.pallas_call(functools.partial(kernel, n, n == 16), out_shape=jax.Shape...]
where the time goes in v2:
time: 43 us; the launch traced here: 42.8 us
  Pallas kernels  41.5 us (97%)
  other arithmetic  1.33 us (3%)
    pallas_call x1, Pallas kernels, shards(): pl.pallas_call(functools.partial(kernel, n, n == 16), out_shape=jax.Shape...  41.5 us
    mul x1, other arithmetic, shards(): return sums * (1.0 / jnp.sqrt(jnp.float32(layers * width * width)))  1.33 us

profile of v2, /device:TPU:1, one launch (start us, length us, event | category | flops | bytes accessed | tf_op | source)
XLA Modules:
  0.0 42.8 jit_solution(16617637844308775161)
XLA Ops:
  0.0 41.5 %influence.1 = f32[16,256]{1,0:T(8,128)} custom-call(bf16[2,256,4096]{2,1,0:T(8,128)(2,1)} %acts.1, bf16[2,256,4096]{2,1,0:T(8,128)(2,1)} %grads.1, bf16[2,64,4096]{2,1,0:T(8,128)(2,1)} %bitcast.2, bf16[2,64,4096]{2,1,0:T(8,128)(2,1)} %bitcast.3, s32[1,256]{1,0:T(1,128)} %ids.1, bf16[2,16,4096]{2,1,0:T(8,128)(2,1)} %queries.1), custom_call_target="tpu_custom_call" | custom-call | tf_op jit(solution)/shard_map/influence/pallas_call | solution.py:301
  41.5 1.3 %broadcast_multiply_fusion = f32[16,256]{1,0:T(8,128)} fusion(f32[16,256]{1,0:T(8,128)} %influence.1), kind=kLoop, calls=%fused_computation | loop fusion | flops 4096 | bytes 32768 | tf_op jit(solution)/shard_map/mul | solution.py:334

commit v3 on v2

--- a/solution.py
+++ b/solution.py
@@ -33,7 +33,7 @@
     n, folded, acts, grads, pin, pout, ids, queries, out,
     abuf, pbuf, qbuf, gram, rsbuf, xbuf, full, xs, rs, outer_t, inner_2, flat,
     load_sem, own_sem, rs_send, rs_recv, x_send, x_recv, ag_send, ag_recv,
-    ring_send, ring_recv, chip_send, chip_recv,
+    ring_send, ring_recv, chip_send, chip_recv, cross_send, cross_recv, last_send, last_recv,
 ):
     layers, tokens, depth = acts.shape
     step_k = 1024
@@ -42,6 +42,19 @@
     chips = n // 2
     half = chips // 2
     chip, core = me // 2, me % 2
+    group = lax.axis_index("group")
+    side_of = group % 2
+    across = group + 1 - 2 * side_of
+    cols = width * width
+    lacking = 128 * ((cols // 128 + 1) // 3)
+    round_cols = cols - lacking
+
+    def columns(start, size):
+        return pl.ds(pl.multiple_of(start, 128), size)
+
+    ring_span = columns(side_of * lacking, round_cols)
+    give_span = columns(side_of * round_cols, lacking)
+    get_span = columns((1 - side_of) * round_cols, lacking)
 
     def pos_to_dev(p):
         p = (p + chips) % chips
@@ -63,6 +76,7 @@
     for k in range(1, n):
         pl.semaphore_signal(barrier, inc=1, device_id={"dp": (me + k) % n}, device_id_type=MESH)
 
+    pl.semaphore_signal(barrier, inc=1, device_id={"group": across, "dp": me}, device_id_type=MESH)
     loads = []
     for layer in range(layers):
         for side, (data, proj) in enumerate(((acts, pin), (grads, pout))):
@@ -77,17 +91,18 @@
     def rows(dev):
         return pl.ds(pl.multiple_of(dev * EX_DEV, EX_DEV), EX_DEV)
 
-    def remote(src, dst, send, recv, dev):
+    def remote(src, dst, send, recv, dev, to_group=None):
         return pltpu.make_async_remote_copy(
             src_ref=src, dst_ref=dst, send_sem=send, recv_sem=recv,
-            device_id={"dp": dev}, device_id_type=MESH,
+            device_id={"group": group if to_group is None else to_group, "dp": dev},
+            device_id_type=MESH,
         )
 
     def ring(step, way, layer, arriving):
         sign = 1 - 2 * way
         origin = pos_to_dev(pos - sign * (step + (1 if arriving else 0)))
-        dst = qbuf.at[layer, rows(origin), :]
-        src = queries.at[layer] if step == 0 and not arriving else dst
+        dst = qbuf.at[layer, rows(origin), ring_span]
+        src = queries.at[layer, :, ring_span] if step == 0 and not arriving else dst
         sems = ring_send.at[way, step, layer], ring_recv.at[way, step, layer]
         return remote(src, dst, *sems, right if way == 0 else left)
 
@@ -101,10 +116,28 @@
         origin = me if step < 0 else pos_to_dev(pos - sign * (step + 1))
         if arriving:
             origin = origin + (1 - 2 * core)
-        dst = qbuf.at[layer, rows(origin), :]
+        dst = qbuf.at[layer, rows(origin), slice(None) if step < 0 else ring_span]
         src = queries.at[layer] if step < 0 and not arriving else dst
         sems = chip_send.at[way, step + 1, layer], chip_recv.at[way, step + 1, layer]
         return remote(src, dst, *sems, partner)
+
+    def cross(step, way, layer, arriving):
+        origin = pos_to_dev(pos - (1 - 2 * way) * (step + 1))
+        dst = qbuf.at[layer, rows(origin), get_span if arriving else give_span]
+        return remote(dst, dst, cross_send.at[way, step, layer], cross_recv.at[way, step, layer], me, across)
+
+    def on_chip_crossed(step, way, layer, arriving):
+        origin = pos_to_dev(pos - (1 - 2 * way) * (step + 1))
+        if arriving:
+            origin = origin + (1 - 2 * core)
+        dst = qbuf.at[layer, rows(origin), get_span]
+        return remote(dst, dst, last_send.at[way, step, layer], last_recv.at[way, step, layer], partner)
+
+    def advance_crossed(step, layer):
+        for way in range(2):
+            if layer in carried(step, way):
+                cross(step, way, layer, True).wait_recv()
+                on_chip_crossed(step, way, layer, False).start()
 
     def advance(step, layer):
         for way in range(2):
@@ -112,6 +145,7 @@
                 ring(step, way, layer, True).wait_recv()
                 if step + 1 < half and layer in carried(step + 1, way):
                     ring(step + 1, way, layer, False).start()
+                cross(step, way, layer, False).start()
                 on_chip(step, way, layer, False).start()
 
     lane = lax.broadcasted_iota(jnp.int32, (1, 2 * width), 1)
@@ -139,7 +173,7 @@
         g = lax.dot_general(both, both, TN, precision=HIGHEST, preferred_element_type=jnp.float32)
         gram[pl.ds(layer * width, width), :] = jnp.where(low, g[:width], g[width:])
 
-    pl.semaphore_wait(barrier, n - 1)
+    pl.semaphore_wait(barrier, n)
     for layer in range(layers):
         for way in range(2):
             ring(0, way, layer, False).start()
@@ -164,7 +198,6 @@
         copy.start()
     mine = gram[pl.ds(pl.multiple_of(8 * slot, 8), 8), :]
     advance(0, 0)
-    advance(0, 1)
     for copy in scatter:
         copy.wait_recv()
     for k in range(1, SLICES):
@@ -190,12 +223,12 @@
     ]
     for copy in gather:
         copy.start()
+    advance(0, 1)
     advance(1, 0)
     for k in range(1, SLICES):
         there = slice_of(full, sources[k])
         remote(there, there, ag_send.at[k], ag_recv.at[k], block + sources[k]).wait_recv()
 
-    advance(1, 1)
     wide = 2 * width
     row = lax.broadcasted_iota(jnp.int32, (wide, wide), 0)
     col = lax.broadcasted_iota(jnp.int32, (wide, wide), 1)
@@ -229,8 +262,12 @@
             rs[layer] = dot(r, r) * up - eye * (up - 1.0)
         return t2
 
-    lax.fori_loop(0, 6, doubling, jnp.float32(2.0 * t * t - 1.0))
+    t = lax.fori_loop(0, 3, doubling, jnp.float32(2.0 * t * t - 1.0))
+    advance(1, 1)
+    lax.fori_loop(0, 3, doubling, t)
     advance(2, 0)
+    advance_crossed(0, 0)
+    advance_crossed(0, 1)
 
     onehot = (ids[...] == lax.broadcasted_iota(jnp.int32, (EX_DEV, tokens), 0)).astype(jnp.float32)
     for layer in range(layers):
@@ -241,6 +278,7 @@
         inner_2[layer, 0], inner_2[layer, 1] = split(twice)
         outer_t[layer] = w.T[width:]
     advance(2, 1)
+    advance_crossed(1, 0)
 
     per = 16
 
@@ -264,23 +302,33 @@
     for step in range(3, half):
         for layer in range(layers):
             advance(step, layer)
+    advance_crossed(1, 1)
     own.wait()
     everything = [(-1, 0, layer) for layer in range(layers)]
     everything += [(step, way, layer) for step in range(half) for way in range(2) for layer in carried(step, way)]
     for item in everything:
         on_chip(*item, True).wait_recv()
+    per_score = round_cols // 3
 
     def score_part(c, total):
-        at = pl.ds(pl.multiple_of(c * step_k, step_k), step_k)
+        at = columns(side_of * lacking + c * per_score, per_score)
         for layer in range(layers):
             total = total + lax.dot_general(
                 flat[layer, :, at], qbuf[layer, :, at], NT, preferred_element_type=jnp.float32
             )
         return total
 
-    total = lax.fori_loop(
-        0, width * width // step_k, score_part, jnp.zeros((2 * EX_DEV, EX_DEV * n), jnp.float32)
-    )
+    for step in range(2, half):
+        for layer in range(layers):
+            advance_crossed(step, layer)
+    total = lax.fori_loop(0, 3, score_part, jnp.zeros((2 * EX_DEV, EX_DEV * n), jnp.float32))
+    for item in everything:
+        if item[0] >= 0:
+            on_chip_crossed(*item, True).wait_recv()
+    for layer in range(layers):
+        total = total + lax.dot_general(
+            flat[layer, :, get_span], qbuf[layer, :, get_span], NT, preferred_element_type=jnp.float32
+        )
     out[...] = total[:EX_DEV] + total[EX_DEV:]
 
     for copy in scatter + crossing + gather:
@@ -288,6 +336,8 @@
     for item in everything:
         if item[0] >= 0:
             ring(*item, False).wait_send()
+            cross(*item, False).wait_send()
+            on_chip_crossed(*item, False).wait_send()
         on_chip(*item, False).wait_send()
 
 
@@ -323,6 +373,8 @@
             dma((SLICES,)), dma((SLICES,)),
             dma((2, half, layers)), dma((2, half, layers)),
             dma((2, half + 1, layers)), dma((2, half + 1, layers)),
+            dma((2, half, layers)), dma((2, half, layers)),
+            dma((2, half, layers)), dma((2, half, layers)),
         ],
         compiler_params=pltpu.CompilerParams(
             collective_id=0, has_side_effects=True, vmem_limit_bytes=60 * 1024 * 1024

time: 43 us -> 41.3 us (0.960)
  Pallas kernels: 41.5 us -> 39.4 us
    pallas_call x1, Pallas kernels: 41.5 us -> 39.4 us  [shards(): pl.pallas_call(functools.partial(kernel, n, n == 16), out_shape=jax.Shape...]
where the time goes in v3:
time: 41.3 us; the launch traced here: 40.7 us
  Pallas kernels  39.4 us (95%)
  other arithmetic  1.33 us (3%)
    pallas_call x1, Pallas kernels, shards(): pl.pallas_call(functools.partial(kernel, n, n == 16), out_shape=jax.Shape...  39.4 us
    mul x1, other arithmetic, shards(): return sums * (1.0 / jnp.sqrt(jnp.float32(layers * width * width)))  1.33 us

profile of v3, /device:TPU:1, one launch (start us, length us, event | category | flops | bytes accessed | tf_op | source)
XLA Modules:
  0.0 40.7 jit_solution(9174520915057545398)
XLA Ops:
  0.0 39.4 %influence.1 = f32[16,256]{1,0:T(8,128)} custom-call(bf16[2,256,4096]{2,1,0:T(8,128)(2,1)} %acts.1, bf16[2,256,4096]{2,1,0:T(8,128)(2,1)} %grads.1, bf16[2,64,4096]{2,1,0:T(8,128)(2,1)} %bitcast.2, bf16[2,64,4096]{2,1,0:T(8,128)(2,1)} %bitcast.3, s32[1,256]{1,0:T(1,128)} %ids.1, bf16[2,16,4096]{2,1,0:T(8,128)(2,1)} %queries.1), custom_call_target="tpu_custom_call" | custom-call | tf_op jit(solution)/shard_map/influence/pallas_call | solution.py:351
  39.4 1.3 %broadcast_multiply_fusion = f32[16,256]{1,0:T(8,128)} fusion(f32[16,256]{1,0:T(8,128)} %influence.1), kind=kLoop, calls=%fused_computation | loop fusion | flops 4096 | bytes 32768 | tf_op jit(solution)/shard_map/mul | solution.py:386

commit v4 on v3

--- a/solution.py
+++ b/solution.py
@@ -52,7 +52,8 @@
     def columns(start, size):
         return pl.ds(pl.multiple_of(start, 128), size)
 
-    ring_span = columns(side_of * lacking, round_cols)
+    middle_span = columns(lacking, cols - 2 * lacking)
+    pieces = 2 * layers
     give_span = columns(side_of * round_cols, lacking)
     get_span = columns((1 - side_of) * round_cols, lacking)
 
@@ -98,27 +99,32 @@
             device_id_type=MESH,
         )
 
-    def ring(step, way, layer, arriving):
+    def span_of(piece):
+        return give_span if piece < layers else middle_span
+
+    def ring(step, way, piece, arriving):
+        layer = piece % layers
         sign = 1 - 2 * way
         origin = pos_to_dev(pos - sign * (step + (1 if arriving else 0)))
-        dst = qbuf.at[layer, rows(origin), ring_span]
-        src = queries.at[layer, :, ring_span] if step == 0 and not arriving else dst
-        sems = ring_send.at[way, step, layer], ring_recv.at[way, step, layer]
+        dst = qbuf.at[layer, rows(origin), span_of(piece)]
+        src = queries.at[layer, :, span_of(piece)] if step == 0 and not arriving else dst
+        sems = ring_send.at[way, step, piece], ring_recv.at[way, step, piece]
         return remote(src, dst, *sems, right if way == 0 else left)
 
     def carried(step, way):
         if step < half - 1:
-            return list(range(layers))
-        return list(range(way, layers, 2))
-
-    def on_chip(step, way, layer, arriving):
+            return list(range(pieces))
+        return list(range(way, pieces, 2))
+
+    def on_chip(step, way, piece, arriving):
         sign = 1 - 2 * way
+        layer = piece % layers
         origin = me if step < 0 else pos_to_dev(pos - sign * (step + 1))
         if arriving:
             origin = origin + (1 - 2 * core)
-        dst = qbuf.at[layer, rows(origin), slice(None) if step < 0 else ring_span]
+        dst = qbuf.at[layer, rows(origin), slice(None) if step < 0 else span_of(piece)]
         src = queries.at[layer] if step < 0 and not arriving else dst
-        sems = chip_send.at[way, step + 1, layer], chip_recv.at[way, step + 1, layer]
+        sems = chip_send.at[way, step + 1, piece], chip_recv.at[way, step + 1, piece]
         return remote(src, dst, *sems, partner)
 
     def cross(step, way, layer, arriving):
@@ -139,14 +145,15 @@
                 cross(step, way, layer, True).wait_recv()
                 on_chip_crossed(step, way, layer, False).start()
 
-    def advance(step, layer):
+    def advance(step, piece):
         for way in range(2):
-            if layer in carried(step, way):
-                ring(step, way, layer, True).wait_recv()
-                if step + 1 < half and layer in carried(step + 1, way):
-                    ring(step + 1, way, layer, False).start()
-                cross(step, way, layer, False).start()
-                on_chip(step, way, layer, False).start()
+            if piece in carried(step, way):
+                ring(step, way, piece, True).wait_recv()
+                if step + 1 < half and piece in carried(step + 1, way):
+                    ring(step + 1, way, piece, False).start()
+                if piece < layers:
+                    cross(step, way, piece, False).start()
+                on_chip(step, way, piece, False).start()
 
     lane = lax.broadcasted_iota(jnp.int32, (1, 2 * width), 1)
     low = lane < width
@@ -174,14 +181,6 @@
         gram[pl.ds(layer * width, width), :] = jnp.where(low, g[:width], g[width:])
 
     pl.semaphore_wait(barrier, n)
-    for layer in range(layers):
-        for way in range(2):
-            ring(0, way, layer, False).start()
-    for layer in range(layers):
-        on_chip(-1, 0, layer, False).start()
-    own = pltpu.make_async_copy(queries, qbuf.at[:, rows(me), :], own_sem)
-    own.start()
-
     slot = me % SLICES
     block = me - slot
 
@@ -196,8 +195,15 @@
     ]
     for copy in scatter:
         copy.start()
+    for piece in range(pieces):
+        for way in range(2):
+            ring(0, way, piece, False).start()
+    for layer in range(layers):
+        on_chip(-1, 0, layer, False).start()
+    own = pltpu.make_async_copy(queries, qbuf.at[:, rows(me), :], own_sem)
+    own.start()
+
     mine = gram[pl.ds(pl.multiple_of(8 * slot, 8), 8), :]
-    advance(0, 0)
     for copy in scatter:
         copy.wait_recv()
     for k in range(1, SLICES):
@@ -223,12 +229,14 @@
     ]
     for copy in gather:
         copy.start()
-    advance(0, 1)
-    advance(1, 0)
+    for piece in range(pieces):
+        advance(0, piece)
     for k in range(1, SLICES):
         there = slice_of(full, sources[k])
         remote(there, there, ag_send.at[k], ag_recv.at[k], block + sources[k]).wait_recv()
 
+    advance(1, 0)
+    advance(1, 1)
     wide = 2 * width
     row = lax.broadcasted_iota(jnp.int32, (wide, wide), 0)
     col = lax.broadcasted_iota(jnp.int32, (wide, wide), 1)
@@ -263,11 +271,13 @@
         return t2
 
     t = lax.fori_loop(0, 3, doubling, jnp.float32(2.0 * t * t - 1.0))
-    advance(1, 1)
+    for piece in range(2, pieces):
+        advance(1, piece)
+    advance_crossed(0, 0)
+    advance_crossed(0, 1)
     lax.fori_loop(0, 3, doubling, t)
     advance(2, 0)
-    advance_crossed(0, 0)
-    advance_crossed(0, 1)
+    advance(2, 1)
 
     onehot = (ids[...] == lax.broadcasted_iota(jnp.int32, (EX_DEV, tokens), 0)).astype(jnp.float32)
     for layer in range(layers):
@@ -277,8 +287,10 @@
         twice = jnp.where(low, w, pltpu.roll(w, width, 1))
         inner_2[layer, 0], inner_2[layer, 1] = split(twice)
         outer_t[layer] = w.T[width:]
-    advance(2, 1)
+    for piece in range(2, pieces):
+        advance(2, piece)
     advance_crossed(1, 0)
+    advance_crossed(1, 1)
 
     per = 16
 
@@ -300,12 +312,11 @@
     lax.fori_loop(0, width // per, example_part, 0)
 
     for step in range(3, half):
-        for layer in range(layers):
-            advance(step, layer)
-    advance_crossed(1, 1)
+        for piece in range(pieces):
+            advance(step, piece)
     own.wait()
     everything = [(-1, 0, layer) for layer in range(layers)]
-    everything += [(step, way, layer) for step in range(half) for way in range(2) for layer in carried(step, way)]
+    everything += [(step, way, piece) for step in range(half) for way in range(2) for piece in carried(step, way)]
     for item in everything:
         on_chip(*item, True).wait_recv()
     per_score = round_cols // 3
@@ -323,7 +334,7 @@
             advance_crossed(step, layer)
     total = lax.fori_loop(0, 3, score_part, jnp.zeros((2 * EX_DEV, EX_DEV * n), jnp.float32))
     for item in everything:
-        if item[0] >= 0:
+        if item[0] >= 0 and item[2] < layers:
             on_chip_crossed(*item, True).wait_recv()
     for layer in range(layers):
         total = total + lax.dot_general(
@@ -336,6 +347,7 @@
     for item in everything:
         if item[0] >= 0:
             ring(*item, False).wait_send()
+        if item[0] >= 0 and item[2] < layers:
             cross(*item, False).wait_send()
             on_chip_crossed(*item, False).wait_send()
         on_chip(*item, False).wait_send()
@@ -371,8 +383,8 @@
             dma((SLICES,)), dma((SLICES,)),
             dma((n // SLICES,)), dma((n // SLICES,)),
             dma((SLICES,)), dma((SLICES,)),
-            dma((2, half, layers)), dma((2, half, layers)),
-            dma((2, half + 1, layers)), dma((2, half + 1, layers)),
+            dma((2, half, 2 * layers)), dma((2, half, 2 * layers)),
+            dma((2, half + 1, 2 * layers)), dma((2, half + 1, 2 * layers)),
             dma((2, half, layers)), dma((2, half, layers)),
             dma((2, half, layers)), dma((2, half, layers)),
         ],

time: 41.3 us -> 38.9 us (0.942)
  Pallas kernels: 39.4 us -> 36.9 us
    pallas_call x1, Pallas kernels: 39.4 us -> 36.9 us  [shards(): pl.pallas_call(functools.partial(kernel, n, n == 16), out_shape=jax.Shape...]
where the time goes in v4:
time: 38.9 us; the launch traced here: 38.2 us
  Pallas kernels  36.9 us (95%)
  other arithmetic  1.33 us (3%)
    pallas_call x1, Pallas kernels, shards(): pl.pallas_call(functools.partial(kernel, n, n == 16), out_shape=jax.Shape...  36.9 us
    mul x1, other arithmetic, shards(): return sums * (1.0 / jnp.sqrt(jnp.float32(layers * width * width)))  1.33 us

profile of v4, /device:TPU:1, one launch (start us, length us, event | category | flops | bytes accessed | tf_op | source)
XLA Modules:
  0.0 38.2 jit_solution(15037505790928240557)
XLA Ops:
  0.0 36.9 %influence.1 = f32[16,256]{1,0:T(8,128)} custom-call(bf16[2,256,4096]{2,1,0:T(8,128)(2,1)} %acts.1, bf16[2,256,4096]{2,1,0:T(8,128)(2,1)} %grads.1, bf16[2,64,4096]{2,1,0:T(8,128)(2,1)} %bitcast.2, bf16[2,64,4096]{2,1,0:T(8,128)(2,1)} %bitcast.3, s32[1,256]{1,0:T(1,128)} %ids.1, bf16[2,16,4096]{2,1,0:T(8,128)(2,1)} %queries.1), custom_call_target="tpu_custom_call" | custom-call | tf_op jit(solution)/shard_map/influence/pallas_call | solution.py:363
  36.9 1.3 %broadcast_multiply_fusion = f32[16,256]{1,0:T(8,128)} fusion(f32[16,256]{1,0:T(8,128)} %influence.1), kind=kLoop, calls=%fused_computation | loop fusion | flops 4096 | bytes 32768 | tf_op jit(solution)/shard_map/mul | solution.py:398

commit v5 on v4

--- a/solution.py
+++ b/solution.py
@@ -179,8 +179,16 @@
         tokens_out.append(both)
         g = lax.dot_general(both, both, TN, precision=HIGHEST, preferred_element_type=jnp.float32)
         gram[pl.ds(layer * width, width), :] = jnp.where(low, g[:width], g[width:])
-
-    pl.semaphore_wait(barrier, n)
+        if layer == 0:
+            pl.semaphore_wait(barrier, n)
+            for piece in range(pieces):
+                for way in range(2):
+                    ring(0, way, piece, False).start()
+            for layer in range(layers):
+                on_chip(-1, 0, layer, False).start()
+            own = pltpu.make_async_copy(queries, qbuf.at[:, rows(me), :], own_sem)
+            own.start()
+
     slot = me % SLICES
     block = me - slot
 
@@ -195,14 +203,6 @@
     ]
     for copy in scatter:
         copy.start()
-    for piece in range(pieces):
-        for way in range(2):
-            ring(0, way, piece, False).start()
-    for layer in range(layers):
-        on_chip(-1, 0, layer, False).start()
-    own = pltpu.make_async_copy(queries, qbuf.at[:, rows(me), :], own_sem)
-    own.start()
-
     mine = gram[pl.ds(pl.multiple_of(8 * slot, 8), 8), :]
     for copy in scatter:
         copy.wait_recv()

time: 38.9 us -> 39.4 us (1.013)
  Pallas kernels: 36.9 us -> 37.4 us
    pallas_call x1, Pallas kernels: 36.9 us -> 37.4 us  [shards(): pl.pallas_call(functools.partial(kernel, n, n == 16), out_shape=jax.Shape...]
where the time goes in v5:
time: 39.4 us; the launch traced here: 38.7 us
  Pallas kernels  37.4 us (95%)
  other arithmetic  1.33 us (3%)
    pallas_call x1, Pallas kernels, shards(): pl.pallas_call(functools.partial(kernel, n, n == 16), out_shape=jax.Shape...  37.4 us
    mul x1, other arithmetic, shards(): return sums * (1.0 / jnp.sqrt(jnp.float32(layers * width * width)))  1.33 us

profile of v5, /device:TPU:1, one launch (start us, length us, event | category | flops | bytes accessed | tf_op | source)
XLA Modules:
  0.0 38.7 jit_solution(12697282700488610210)
XLA Ops:
  0.0 37.4 %influence.1 = f32[16,256]{1,0:T(8,128)} custom-call(bf16[2,256,4096]{2,1,0:T(8,128)(2,1)} %acts.1, bf16[2,256,4096]{2,1,0:T(8,128)(2,1)} %grads.1, bf16[2,64,4096]{2,1,0:T(8,128)(2,1)} %bitcast.2, bf16[2,64,4096]{2,1,0:T(8,128)(2,1)} %bitcast.3, s32[1,256]{1,0:T(1,128)} %ids.1, bf16[2,16,4096]{2,1,0:T(8,128)(2,1)} %queries.1), custom_call_target="tpu_custom_call" | custom-call | tf_op jit(solution)/shard_map/influence/pallas_call | solution.py:363
  37.4 1.3 %broadcast_multiply_fusion = f32[16,256]{1,0:T(8,128)} fusion(f32[16,256]{1,0:T(8,128)} %influence.1), kind=kLoop, calls=%fused_computation | loop fusion | flops 4096 | bytes 32768 | tf_op jit(solution)/shard_map/mul | solution.py:398
